TPU v7x, 32 devices: a whole 2x2x4 slice. The times are simulated.
32 devices in a mesh: dp: 8 (over z, x), tensor: 4 (over y, core).
Axes of the slice: x: 2, y: 2, z: 4, core: 2. Of those that a mesh axis runs over, the one named last changes fastest.
Arguments:
- tokens_in: bfloat16 [12288, 768], P('dp'), may hold values from -6 to 6
- cotangent: bfloat16 [12288, 768], P('dp'), may hold values from -6 to 6
- span_mask: int32 [12288], P('dp'), may hold values from 0 to 1, as said below
- lengths: int32 [24], P('dp'), may hold values from 128 to 512, as said below
- step: int32 [1], replicated, may hold values from 1000 to 31999
- warmup: int32 [1], replicated, may hold values from 1000 to 29999
- total: int32 [1], replicated, may hold values from 32000 to 40000
- w_qkv: float32 [768, 3, 768], P(None, None, 'tensor'), may hold values from -0.21875 to 0.21875
- w_out: float32 [768, 768], P(None, 'tensor'), may hold values from -1.25 to 1.25
- w_in: float32 [768, 3072], P(None, 'tensor'), may hold values from -0.21875 to 0.21875
- w_back: float32 [768, 3072], P(None, 'tensor'), may hold values from -0.109375 to 0.109375
- gains: float32 [2, 768], replicated, may hold values from 0.5 to 1.5
- biases: float32 [6, 768], replicated, may hold values from -3 to 3
- bias_in: float32 [3072], replicated, may hold values from -3 to 3
- mom_qkv: float32 [2, 768, 3, 768], P(None, 'dp', None, 'tensor'), as said below
- mom_out: float32 [2, 768, 768], P(None, 'dp', 'tensor'), as said below
- mom_in: float32 [2, 768, 3072], P(None, 'dp', 'tensor'), as said below
- mom_back: float32 [2, 768, 3072], P(None, 'dp', 'tensor'), as said below
- mom_gains: float32 [2, 2, 768], replicated, as said below
- mom_biases: float32 [2, 6, 768], replicated, as said below
- mom_bias_in: float32 [2, 3072], replicated, as said below
Outputs:
- normed_out: bfloat16 [12288, 768], P('dp')
- input_grad: float32 [12288, 768], P('dp')
- change_qkv: float32 [768, 3, 768], P(None, None, 'tensor')
- change_out_proj: float32 [768, 768], P(None, 'tensor')
- change_in_proj: float32 [768, 3072], P(None, 'tensor')
- change_back_proj: float32 [768, 3072], P(None, 'tensor')
- change_gains: float32 [2, 768], replicated
- change_biases: float32 [6, 768], replicated
- change_bias_in: float32 [3072], replicated
- new_mom_qkv: float32 [2, 768, 3, 768], P(None, 'dp', None, 'tensor')
- new_mom_out: float32 [2, 768, 768], P(None, 'dp', 'tensor')
- new_mom_in: float32 [2, 768, 3072], P(None, 'dp', 'tensor')
- new_mom_back: float32 [2, 768, 3072], P(None, 'dp', 'tensor')
- new_mom_gains: float32 [2, 2, 768], replicated
- new_mom_biases: float32 [2, 6, 768], replicated
- new_mom_bias_in: float32 [2, 3072], replicated
Inputs may be any that keep to these rules, and one draw needn't show every extreme that they name: `span_mask`: marked positions lie below their sequence's length and form unions of spans of 1 to 10 positions; each sequence has at most 76 of them, and in every draw each of the 3 sequences of some index of dp has exactly 76. `lengths`: a sequence's real tokens stand at its start, the rest is padding. step < total. warmup < total. `mom_qkv`: index 1 of the leading dimension holds positive second moments. `mom_out`: index 1 of the leading dimension holds positive second moments. `mom_in`: index 1 of the leading dimension holds positive second moments. `mom_back`: index 1 of the leading dimension holds positive second moments. `mom_gains`: index 1 of the leading dimension holds positive second moments. `mom_biases`: index 1 of the leading dimension holds positive second moments. `mom_bias_in`: index 1 of the leading dimension holds positive second moments.
All inputs are finite; a program needn't handle non-finite values.
Results may differ from a plain program's by a relative error of at most 0.017.
The roundings to bfloat16 on the way count: a program that leaves them out, or rounds other values in their place, can miss the bound.
Values sent between devices are 32-bit elements; how exact they have to be, the bound alone decides.
A program may use at most 128 MiB of HBM per device.

v0:
```python
import math
import jax
import jax.numpy as jnp
from jax import lax
from jax.sharding import PartitionSpec as P

HD = 64
SPAN_ROWS = 80
NORM_EPS = 1e-12
BETA_ONE = 0.9
BETA_TWO = 0.999
ADAM_EPS = 1e-06
WEIGHT_DECAY = 0.01


def layer_norm(values, gain, shift):
    center = values - jnp.mean(values, axis=-1, keepdims=True)
    spread = jnp.mean(center * center, axis=-1, keepdims=True)
    return center * lax.rsqrt(spread + NORM_EPS) * gain + shift


def exact_gelu(values):
    return jax.nn.gelu(values, approximate=False)


def outer_sum(left, right):
    return jnp.einsum("ta,tb->ab", left, right, preferred_element_type=jnp.float32)


def adam_step(weight, grad, moments, ratio, corr_one, corr_two, decay):
    first = BETA_ONE * moments[0] + (1.0 - BETA_ONE) * grad
    second = BETA_TWO * moments[1] + (1.0 - BETA_TWO) * grad * grad
    update = first / corr_one / (jnp.sqrt(second / corr_two) + ADAM_EPS) + decay * weight
    return (-ratio * update, jnp.stack([first, second]))


def on_device(
    tokens_in,
    cotangent,
    span_mask,
    lengths,
    step,
    warmup,
    total,
    w_qkv,
    w_out,
    w_in,
    w_back,
    gains,
    biases,
    bias_in,
    mom_qkv,
    mom_out,
    mom_in,
    mom_back,
    mom_gains,
    mom_biases,
    mom_bias_in,
):
    row_count, model_width = tokens_in.shape
    seq_count = lengths.shape[0]
    seq_length = row_count // seq_count
    head_cols = w_qkv.shape[2]
    hidden_cols = w_in.shape[1]
    head_size = HD
    local_heads = head_cols // head_size
    query_scale = 1.0 / math.sqrt(head_size)
    tensor_slot = lax.axis_index("tensor")
    bias_query = lax.dynamic_slice_in_dim(biases[0], tensor_slot * head_cols, head_cols)
    bias_value = lax.dynamic_slice_in_dim(biases[1], tensor_slot * head_cols, head_cols)
    bias_hidden = lax.dynamic_slice_in_dim(bias_in, tensor_slot * hidden_cols, hidden_cols)
    qkv_low = w_qkv.astype(jnp.bfloat16).reshape(model_width, 3 * head_cols)
    out_low = w_out.astype(jnp.bfloat16)
    in_low = w_in.astype(jnp.bfloat16)
    down_low = w_back.astype(jnp.bfloat16)
    projected = jnp.dot(tokens_in, qkv_low, preferred_element_type=jnp.float32).reshape(
        row_count, 3, head_cols
    )
    attn_shape = (seq_count, seq_length, local_heads, head_size)
    queries = (
        ((projected[:, 0] + bias_query) * query_scale).astype(jnp.bfloat16).reshape(attn_shape)
    )
    keys = projected[:, 1].astype(jnp.bfloat16).reshape(attn_shape)
    values = (projected[:, 2] + bias_value).astype(jnp.bfloat16).reshape(attn_shape)
    positions = jnp.arange(seq_length, dtype=jnp.int32)
    inside = positions[None, :] < lengths[:, None]
    key_bias = jnp.where(inside, 0.0, -1000000000.0).astype(jnp.float32)

    def score_block():
        raw = jnp.einsum("sqhd,skhd->shqk", queries, keys, preferred_element_type=jnp.float32)
        return raw + key_bias[:, None, None, :]

    scores = score_block()
    peak = jnp.max(scores, axis=-1, keepdims=True)
    log_total = peak + jnp.log(jnp.sum(jnp.exp(scores - peak), axis=-1, keepdims=True))
    probs_low = jnp.exp(scores - log_total).astype(jnp.bfloat16)
    context_low = (
        jnp.einsum("shqk,skhd->sqhd", probs_low, values, preferred_element_type=jnp.float32)
        .reshape(row_count, head_cols)
        .astype(jnp.bfloat16)
    )
    attn_part = jnp.einsum("tc,dc->td", context_low, out_low, preferred_element_type=jnp.float32)
    attn_sum = lax.psum(attn_part, "tensor")
    residual_one = tokens_in.astype(jnp.float32) + attn_sum + biases[2]
    normed = layer_norm(residual_one, gains[0], biases[3])
    normed_low = normed.astype(jnp.bfloat16)
    pre_act = jnp.dot(normed_low, in_low, preferred_element_type=jnp.float32) + bias_hidden
    act_low = exact_gelu(pre_act).astype(jnp.bfloat16)
    down_part = jnp.einsum("tf,df->td", act_low, down_low, preferred_element_type=jnp.float32)
    down_sum = lax.psum(down_part, "tensor")
    residual_two = normed + down_sum + biases[4]
    live = inside.astype(jnp.int32) * span_mask.reshape(seq_count, seq_length) > 0
    upto = (positions[:, None] <= positions[None, :]).astype(jnp.float32)
    rank = jnp.dot(live.astype(jnp.float32), upto).astype(jnp.int32) - 1
    slots = jnp.arange(SPAN_ROWS, dtype=jnp.int32)
    pick = (live[:, None, :] & (rank[:, None, :] == slots[None, :, None])).astype(jnp.float32)
    pick_low = pick.astype(jnp.bfloat16)

    def rows_of(values):
        width = values.shape[-1]
        return jnp.einsum(
            "srt,std->srd",
            pick,
            values.reshape(seq_count, seq_length, width),
            precision=lax.Precision.HIGHEST,
        ).reshape(seq_count * SPAN_ROWS, width)

    def low_rows_of(values):
        width = values.shape[-1]
        return jnp.einsum(
            "srt,std->srd",
            pick_low,
            values.reshape(seq_count, seq_length, width),
            preferred_element_type=jnp.bfloat16,
        ).reshape(seq_count * SPAN_ROWS, width)

    result = layer_norm(residual_two, gains[1], biases[5])
    normed_out = result.astype(jnp.bfloat16)
    residual_one_rows = rows_of(residual_one)
    residual_two_rows = rows_of(residual_two)
    grad_result = low_rows_of(cotangent).astype(jnp.float32)
    _, norm_two_back = jax.vjp(layer_norm, residual_two_rows, gains[1], biases[5])
    d_res_two, d_gain_two, d_shift_two = norm_two_back(grad_result)
    d_res_two_low = d_res_two.astype(jnp.bfloat16)
    normed_low_rows = low_rows_of(normed_low)
    pre_rows = jnp.dot(normed_low_rows, in_low, preferred_element_type=jnp.float32) + bias_hidden
    act_rows, gelu_back = jax.vjp(exact_gelu, pre_rows)
    grad_back = outer_sum(d_res_two_low, act_rows.astype(jnp.bfloat16))
    d_act = jnp.dot(d_res_two_low, down_low, preferred_element_type=jnp.float32)
    d_pre = gelu_back(d_act)[0]
    d_pre_low = d_pre.astype(jnp.bfloat16)
    grad_in = outer_sum(normed_low_rows, d_pre_low)
    d_normed_part = jnp.einsum("tf,df->td", d_pre_low, in_low, preferred_element_type=jnp.float32)
    d_normed = lax.psum(d_normed_part, "tensor") + d_res_two
    _, norm_one_back = jax.vjp(layer_norm, residual_one_rows, gains[0], biases[3])
    d_res_one, d_gain_one, d_shift_one = norm_one_back(d_normed)
    d_res_one_low = d_res_one.astype(jnp.bfloat16)
    grad_out_proj = outer_sum(d_res_one_low, low_rows_of(context_low))
    row_shape = (seq_count, SPAN_ROWS, local_heads, head_size)
    d_context = (
        jnp.dot(d_res_one_low, out_low, preferred_element_type=jnp.float32)
        .astype(jnp.bfloat16)
        .reshape(row_shape)
    )
    query_rows = low_rows_of(queries.reshape(row_count, head_cols)).reshape(row_shape)
    raw = jnp.einsum("sqhd,skhd->shqk", query_rows, keys, preferred_element_type=jnp.float32)
    probs = jax.nn.softmax(raw + key_bias[:, None, None, :], axis=-1)
    probs_again = probs.astype(jnp.bfloat16)
    d_probs = jnp.einsum("sqhd,skhd->shqk", d_context, values, preferred_element_type=jnp.float32)
    d_values = jnp.einsum(
        "shqk,sqhd->skhd", probs_again, d_context, preferred_element_type=jnp.float32
    ).reshape(row_count, head_cols)
    d_scores = (probs * (d_probs - jnp.sum(probs * d_probs, axis=-1, keepdims=True))).astype(
        jnp.bfloat16
    )
    d_queries = (
        jnp.einsum("shqk,skhd->sqhd", d_scores, keys, preferred_element_type=jnp.float32).reshape(
            seq_count * SPAN_ROWS, head_cols
        )
        * query_scale
    )
    d_keys = jnp.einsum(
        "shqk,sqhd->skhd", d_scores, query_rows, preferred_element_type=jnp.float32
    ).reshape(row_count, head_cols)

    def spread(row_values):
        width = row_values.shape[-1]
        return jnp.einsum(
            "srt,srd->std",
            pick,
            row_values.reshape(seq_count, SPAN_ROWS, width),
            precision=lax.Precision.HIGHEST,
        ).reshape(row_count, width)

    d_proj_low = (
        jnp.stack([spread(d_queries), d_keys, d_values], axis=1)
        .astype(jnp.bfloat16)
        .reshape(row_count, 3 * head_cols)
    )
    grad_qkv = outer_sum(tokens_in, d_proj_low).reshape(model_width, 3, head_cols)
    d_entry_part = jnp.einsum("tc,dc->td", d_proj_low, qkv_low, preferred_element_type=jnp.float32)
    input_grad = lax.psum(d_entry_part, "tensor") + spread(d_res_one)
    first_rank = (tensor_slot == 0).astype(jnp.float32)
    width_zero = jnp.zeros((model_width,), jnp.float32)

    def place_heads(partial_sum):
        return lax.dynamic_update_slice_in_dim(width_zero, partial_sum, tensor_slot * head_cols, 0)

    grad_gains = jnp.stack([d_gain_one, d_gain_two]) * first_rank
    grad_biases = jnp.stack(
        [
            place_heads(jnp.sum(d_queries, axis=0)),
            place_heads(jnp.sum(d_values, axis=0)),
            jnp.sum(d_res_one, axis=0) * first_rank,
            d_shift_one * first_rank,
            jnp.sum(d_res_two, axis=0) * first_rank,
            d_shift_two * first_rank,
        ]
    )
    grad_bias_in = lax.dynamic_update_slice_in_dim(
        jnp.zeros(bias_in.shape, jnp.float32), jnp.sum(d_pre, axis=0), tensor_slot * hidden_cols, 0
    )
    grad_gains, grad_biases, grad_bias_in = lax.psum(
        (grad_gains, grad_biases, grad_bias_in), ("dp", "tensor")
    )
    data_slot = lax.axis_index("dp")
    shard_rows = model_width // lax.axis_size("dp")
    owned = tuple(
        (
            lax.psum_scatter(part, "dp", scatter_dimension=0, tiled=True)
            for part in (grad_qkv, grad_out_proj, grad_in, grad_back)
        )
    )
    clock = step[0].astype(jnp.float32)
    warm = warmup[0].astype(jnp.float32)
    horizon = total[0].astype(jnp.float32)
    ratio = jnp.minimum(clock / warm, (horizon - clock) / (horizon - warm))
    corr_one = 1.0 - jnp.power(BETA_ONE, clock)
    corr_two = 1.0 - jnp.power(BETA_TWO, clock)
    change_rows = []
    fresh_moments = []
    for weight, grad_rows, moment in zip(
        (w_qkv, w_out, w_in, w_back), owned, (mom_qkv, mom_out, mom_in, mom_back)
    ):
        weight_rows = lax.dynamic_slice_in_dim(weight, data_slot * shard_rows, shard_rows, 0)
        row_change, new_moment = adam_step(
            weight_rows, grad_rows, moment, ratio, corr_one, corr_two, WEIGHT_DECAY
        )
        change_rows.append(row_change)
        fresh_moments.append(new_moment)
    change_qkv, change_out_proj, change_in_proj, change_back_proj = (
        lax.all_gather(change_rows[0], "dp", axis=0, tiled=True),
        lax.all_gather(change_rows[1], "dp", axis=0, tiled=True),
        lax.all_gather(change_rows[2], "dp", axis=0, tiled=True),
        lax.all_gather(change_rows[3], "dp", axis=0, tiled=True),
    )
    change_gains, new_mom_gains = adam_step(
        gains, grad_gains, mom_gains, ratio, corr_one, corr_two, 0.0
    )
    change_biases, new_mom_biases = adam_step(
        biases, grad_biases, mom_biases, ratio, corr_one, corr_two, 0.0
    )
    change_bias_in, new_mom_bias_in = adam_step(
        bias_in, grad_bias_in, mom_bias_in, ratio, corr_one, corr_two, 0.0
    )
    return (
        normed_out,
        input_grad,
        change_qkv,
        change_out_proj,
        change_in_proj,
        change_back_proj,
        change_gains,
        change_biases,
        change_bias_in,
        fresh_moments[0],
        fresh_moments[1],
        fresh_moments[2],
        fresh_moments[3],
        new_mom_gains,
        new_mom_biases,
        new_mom_bias_in,
    )


def solution(mesh):
    in_specs = (
        P("dp", None),
        P("dp", None),
        P("dp"),
        P("dp"),
        P(),
        P(),
        P(),
        P(None, None, "tensor"),
        P(None, "tensor"),
        P(None, "tensor"),
        P(None, "tensor"),
        P(),
        P(),
        P(),
        P(None, "dp", None, "tensor"),
        P(None, "dp", "tensor"),
        P(None, "dp", "tensor"),
        P(None, "dp", "tensor"),
        P(),
        P(),
        P(),
    )
    out_specs = (
        P("dp", None),
        P("dp", None),
        P(None, None, "tensor"),
        P(None, "tensor"),
        P(None, "tensor"),
        P(None, "tensor"),
        P(),
        P(),
        P(),
        P(None, "dp", None, "tensor"),
        P(None, "dp", "tensor"),
        P(None, "dp", "tensor"),
        P(None, "dp", "tensor"),
        P(),
        P(),
        P(),
    )
    return jax.shard_map(
        on_device, mesh=mesh, in_specs=in_specs, out_specs=out_specs, check_vma=False
    )
```

profile of v0, /device:TPU:0, one launch (start us, length us, event | category | flops | bytes accessed | tf_op | source)
XLA Modules:
  0.0 894.0 jit_solution(5073173420024962855)
XLA Ops:
  34.5 5.7 fusion.20
  46.6 94.5 %all-reduce.6.cloned.1.call-done = f32[1536,768]{1,0:T(8,128)} async-done(((f32[1536,768]{1,0:T(8,128)}), f32[1536,768]{1,0:T(8,128)}) %all-reduce.6.cloned.1.call-update) | async-done | bytes 4718608 | tf_op jit(solution)/shard_map/psum | solution.py:103
  149.2 17.8 %fusion.18 = f32[1536,768]{1,0:T(8,128)} fusion(bf16[1536,768]{1,0:T(8,128)(2,1)} %fusion.14, f32[768]{0:T(1024)} %dynamic_slice.23, f32[768,768]{1,0:T(8,128)} %param.31, f32[768,768]{1,0:T(8,128)} %param.30), kind=kOutput, calls=%fused_computation.39 | convolution fusion | flops 3702915072 | bytes 11799552 | tf_op jit(solution)/shard_map/tf,df->td/dot_general | solution.py:109
  175.7 4.6 fusion.173
  183.3 78.0 %all-reduce.8.cloned.1.call-done = f32[1536,768]{1,0:T(8,128)} async-done(((f32[1536,768]{1,0:T(8,128)}), f32[1536,768]{1,0:T(8,128)}) %all-reduce.8.cloned.1.call-update) | async-done | bytes 4718608 | tf_op jit(solution)/shard_map/psum | solution.py:110
  261.3 5.3 fusion.166
  276.3 4.8 fusion.180
  283.3 33.8 %all-reduce.10.cloned.1.call-done = f32[240,768]{1,0:T(8,128)} async-done(((f32[240,768]{1,0:T(8,128)}), f32[240,768]{1,0:T(8,128)}) %all-reduce.10.cloned.1.call-update) | async-done | bytes 737296 | tf_op jit(solution)/shard_map/psum | solution.py:154
  339.3 4.4 fusion.181
  348.8 4.6 fusion.62
  355.3 6.1 convolution_bitcast_fusion
  365.0 51.3 %reduce-scatter.5.cloned.1.call-done = f32[96,3,192]{2,0,1:T(8,128)} async-done(((f32[768,3,192]{2,0,1:T(8,128)}), f32[96,3,192]{2,0,1:T(8,128)}) %reduce-scatter.5.cloned.1.call-update) | async-done | bytes 221200 | tf_op jit(solution)/shard_map/reduce_scatter | solution.py:230
  418.5 69.8 %reduce-scatter.9.cloned.1.call-done = f32[96,768]{1,0:T(8,128)} async-done(((f32[768,768]{1,0:T(8,128)}), f32[96,768]{1,0:T(8,128)}) %reduce-scatter.9.cloned.1.call-update) | async-done | bytes 294928 | tf_op jit(solution)/shard_map/reduce_scatter | solution.py:230
  495.9 4.2 add_convert_fusion
  500.1 59.7 %reduce-scatter.11.cloned.1.call-done = f32[96,768]{1,0:T(8,128)} async-done(((f32[768,768]{1,0:T(8,128)}), f32[96,768]{1,0:T(8,128)}) %reduce-scatter.11.cloned.1.call-update) | async-done | bytes 294928 | tf_op jit(solution)/shard_map/reduce_scatter | solution.py:230
  562.9 40.3 %all-reduce = (f32[2,768]{1,0:T(2,128)S(1)}, f32[6,768]{1,0:T(8,128)S(1)}, f32[3072]{0:T(1024)S(1)}) all-reduce(f32[2,768]{1,0:T(2,128)S(1)} %maximum_multiply_fusion, f32[6,768]{1,0:T(8,128)S(1)} %stack.88, f32[3072]{0:T(1024)S(1)} %dynamic_update_slice.13), channel_id=1, replica_groups=mesh['dp'=8,'tensor'=4] {'dp','tensor'}, use_global_device_ids=true, to_apply=%region_27.28 | all-reduce | flops 9216 | bytes 73728 | tf_op jit(solution)/shard_map/psum | solution.py:223
  607.0 4.3 fusion.47
  611.3 13.9 %reduce-scatter.7.cloned.1.call-done = f32[96,192]{1,0:T(8,128)} async-done(((f32[768,192]{1,0:T(8,128)}), f32[96,192]{1,0:T(8,128)}) %reduce-scatter.7.cloned.1.call-update) | async-done | bytes 73744 | tf_op jit(solution)/shard_map/reduce_scatter | solution.py:230
  626.3 32.2 %all_gather.13 = f32[768,192]{1,0:T(8,128)S(1)} all-gather(f32[96,192]{1,0:T(8,128)S(1)} %get-tuple-element.107), channel_id=1, replica_groups=mesh['dp'=8,'tensor'=4] {'dp'}, dimensions={0}, use_global_device_ids=true | all-gather | bytes 663552 | tf_op jit(solution)/shard_map/all_gather | solution.py:253
  660.3 60.5 %all-reduce.12.cloned.1.call-done = f32[1536,768]{1,0:T(8,128)} async-done(((f32[1536,768]{1,0:T(8,128)}), f32[1536,768]{1,0:T(8,128)}) %all-reduce.12.cloned.1.call-update) | async-done | bytes 4718608 | tf_op jit(solution)/shard_map/psum | solution.py:202
  720.8 6.6 bitcast_add_fusion
  729.9 46.0 %all-gather.4.cloned.1.call-done = f32[768,3,192]{2,0,1:T(8,128)} async-done(((f32[96,3,192]{2,0,1:T(8,128)}), f32[768,3,192]{2,0,1:T(8,128)}) %all-gather.4.cloned.1.call-update) | async-done | bytes 1769488 | tf_op jit(solution)/shard_map/all_gather | solution.py:252
  778.8 50.6 %all-gather.6.cloned.1.call-done = f32[768,768]{1,0:T(8,128)} async-done(((f32[96,768]{1,0:T(8,128)}), f32[768,768]{1,0:T(8,128)}) %all-gather.6.cloned.1.call-update) | async-done | bytes 2359312 | tf_op jit(solution)/shard_map/all_gather | solution.py:254
  829.4 53.1 %all-gather.8.cloned.1.call-done = f32[768,768]{1,0:T(8,128)} async-done(((f32[96,768]{1,0:T(8,128)}), f32[768,768]{1,0:T(8,128)}) %all-gather.8.cloned.1.call-update) | async-done | bytes 2359312 | tf_op jit(solution)/shard_map/all_gather | solution.py:255
  (277 shorter events, 124.9 us)
Async XLA Ops:
  7.2 263.8 %copy-start = (bf16[1536,768]{1,0:T(8,128)(2,1)S(1)}, bf16[1536,768]{1,0:T(8,128)(2,1)}, u32[]{:S(2)}) copy-start(bf16[1536,768]{1,0:T(8,128)(2,1)} %param.22) | copy-start | bytes 7077892
  7.2 133.9 %all-reduce.6.cloned.1.call-start = ((), (), s32[]{:S(2)}) async-start(), calls=%async_computation.4 | async-start | bytes 9437184 | tf_op jit(solution)/shard_map/psum | solution.py:103
  44.2 217.1 %all-reduce.8.cloned.1.call-start = ((), (), s32[]{:S(2)}) async-start(), calls=%async_computation.5 | async-start | bytes 9437184 | tf_op jit(solution)/shard_map/psum | solution.py:110
  167.0 150.0 %all-reduce.10.cloned.1.call-start = ((), (), s32[]{:S(2)}) async-start(), calls=%async_computation.6 | async-start | bytes 1474560 | tf_op jit(solution)/shard_map/psum | solution.py:154
  282.5 133.8 %reduce-scatter.5.cloned.1.call-start = ((), (), s32[]{:S(2)}) async-start(), calls=%async_computation.8 | async-start | bytes 2654208 | tf_op jit(solution)/shard_map/reduce_scatter | solution.py:230
  346.7 141.6 %reduce-scatter.9.cloned.1.call-start = ((), (), s32[]{:S(2)}) async-start(), calls=%async_computation.11 | async-start | bytes 2654208 | tf_op jit(solution)/shard_map/reduce_scatter | solution.py:230
  348.8 211.1 %reduce-scatter.11.cloned.1.call-start = ((), (), s32[]{:S(2)}) async-start(), calls=%async_computation.13 | async-start | bytes 2654208 | tf_op jit(solution)/shard_map/reduce_scatter | solution.py:230
  353.4 271.8 %reduce-scatter.7.cloned.1.call-start = ((), (), s32[]{:S(2)}) async-start(), calls=%async_computation.10 | async-start | bytes 884736 | tf_op jit(solution)/shard_map/reduce_scatter | solution.py:230
  355.0 365.8 %all-reduce.12.cloned.1.call-start = ((), (), s32[]{:S(2)}) async-start(), calls=%async_computation.7 | async-start | bytes 9437184 | tf_op jit(solution)/shard_map/psum | solution.py:202
  361.3 130.4 %copy-start.38 = (f32[2,6,768]{2,0,1:T(2,128)S(1)}, f32[2,6,768]{2,0,1:T(2,128)}, u32[]{:S(2)}) copy-start(f32[2,6,768]{2,0,1:T(2,128)} %param.40) | copy-start | bytes 110596
  361.3 130.4 %copy-start.42 = (f32[2,3072]{1,0:T(2,128)S(1)}, f32[2,3072]{1,0:T(2,128)}, u32[]{:S(2)}) copy-start(f32[2,3072]{1,0:T(2,128)} %param.41) | copy-start | bytes 73732
  361.3 131.0 %copy-start.7 = (f32[3,80,768]{2,1,0:T(8,128)S(1)}, f32[3,80,768]{2,1,0:T(8,128)}, u32[]{:S(2)}) copy-start(f32[3,80,768]{2,1,0:T(8,128)} %get-tuple-element.137) | copy-start | bytes 2211844
  361.3 131.0 %copy-start.46 = (f32[3,80]{1,0:T(4,128)S(1)}, f32[3,80]{1,0:T(4,128)}, u32[]{:S(2)}) copy-start(f32[3,80]{1,0:T(4,128)} %copy-done.45) | copy-start | bytes 2884
  361.3 131.0 %copy-start.48 = (f32[3,80]{1,0:T(4,128)S(1)}, f32[3,80]{1,0:T(4,128)}, u32[]{:S(2)}) copy-start(f32[3,80]{1,0:T(4,128)} %copy-done.47) | copy-start | bytes 2884
  361.3 131.0 %copy-start.50 = (f32[3,80]{1,0:T(4,128)S(1)}, f32[3,80]{1,0:T(4,128)}, u32[]{:S(2)}) copy-start(f32[3,80]{1,0:T(4,128)} %copy-done.49) | copy-start | bytes 2884
  361.4 131.4 %copy-start.41 = (f32[1536]{0:T(1024)S(1)}, f32[1536]{0:T(1024)}, u32[]{:S(2)}) copy-start(f32[1536]{0:T(1024)} %get-tuple-element.88) | copy-start | bytes 18436
  361.4 414.5 %all-gather.4.cloned.1.call-start = ((), (), s32[]{:S(2)}) async-start(), calls=%async_computation.9 | async-start | bytes 2654208 | tf_op jit(solution)/shard_map/all_gather | solution.py:252
  418.5 410.9 %all-gather.6.cloned.1.call-start = ((), (), s32[]{:S(2)}) async-start(), calls=%async_computation.12 | async-start | bytes 2654208 | tf_op jit(solution)/shard_map/all_gather | solution.py:254
  490.5 392.0 %all-gather.8.cloned.1.call-start = ((), (), s32[]{:S(2)}) async-start(), calls=%async_computation.14 | async-start | bytes 2654208 | tf_op jit(solution)/shard_map/all_gather | solution.py:255
  495.9 108.7 %copy-start.43 = (f32[2,768]{1,0:T(2,128)S(1)}, f32[2,768]{1,0:T(2,128)}, u32[]{:S(2)}) copy-start(f32[2,768]{1,0:T(2,128)} %param.32) | copy-start | bytes 18436
  495.9 108.7 %copy-start.58 = (f32[2,2,768]{2,1,0:T(2,128)S(1)}, f32[2,2,768]{2,1,0:T(2,128)}, u32[]{:S(2)}) copy-start(f32[2,2,768]{2,1,0:T(2,128)} %param.39) | copy-start | bytes 36868
  495.9 109.9 %copy-start.36 = (f32[1,3072]{1,0:T(1,128)S(1)}, f32[1,3072]{1,0:T(1,128)}, u32[]{:S(2)}) copy-start(f32[1,3072]{1,0:T(1,128)} %get-tuple-element.113) | copy-start | bytes 36868
  495.9 109.9 %copy-start.37 = (f32[1,3072]{1,0:T(1,128)S(1)}, f32[1,3072]{1,0:T(1,128)}, u32[]{:S(2)}) copy-start(f32[1,3072]{1,0:T(1,128)} %get-tuple-element.114) | copy-start | bytes 36868
  495.9 109.9 %copy-start.44 = (f32[3072]{0:T(1024)S(1)}, f32[3072]{0:T(1024)}, u32[]{:S(2)}) copy-start(f32[3072]{0:T(1024)} %param.34) | copy-start | bytes 36868
  (51 other events, 1249.5 us)
Sparse Core Ops, SparseCore 0:
  44.3 96.7 all-reduce.5
  167.1 94.1 all-reduce.7
  282.6 34.3 all-reduce.9
  346.9 69.3 reduce-scatter.4
  420.2 68.0 reduce-scatter.8
  491.6 68.1 reduce-scatter.10
  563.7 61.4 reduce-scatter.6
  627.8 92.9 all-reduce.11
  723.8 52.0 all-gather.3
  778.8 50.5 all-gather.5
  831.8 50.5 all-gather.7
where the time goes:
time: 903 us; the launch traced here: 894 us
  waiting for transfers between devices  611 us (68%)
  matrix products  86.9 us (10%)
  blocking collectives  72.5 us (8%)
  other arithmetic  56.1 us (6%)
  local copies, waits for them, and re-layouts  48.5 us (5%)
  between operations  17.2 us (2%)
    reduce_scatter x4, waiting for transfers between devices, on_device(): lax.psum_scatter(part, 'dp', scatter_dimension=0, tiled=True)  195 us
    psum x1, waiting for transfers between devices, on_device(): attn_sum = lax.psum(attn_part, 'tensor')  94.5 us
    psum x1, waiting for transfers between devices, on_device(): down_sum = lax.psum(down_part, 'tensor')  78 us
    psum x1, waiting for transfers between devices, on_device(): input_grad = lax.psum(d_entry_part, 'tensor') + spread(d_res_one)  60.5 us
    all_gather x1, waiting for transfers between devices, on_device(): lax.all_gather(change_rows[3], 'dp', axis=0, tiled=True)  53.1 us
    all_gather x1, waiting for transfers between devices, on_device(): lax.all_gather(change_rows[2], 'dp', axis=0, tiled=True)  50.6 us
    all_gather x1, waiting for transfers between devices, on_device(): lax.all_gather(change_rows[0], 'dp', axis=0, tiled=True)  46 us
    psum x1, blocking collectives, on_device(): lax.psum((grad_gains, grad_biases, grad_bias_in), ('dp', 'tensor'))  40.3 us
  transfers between devices with their start and end apart: 11, of which 11 were waited for; matrix products, arithmetic and copies ran while one was open for 8% of the time, Pallas kernels for 0%

commit v1 on v0

--- a/solution.py
+++ b/solution.py
@@ -100,7 +100,7 @@
         .astype(jnp.bfloat16)
     )
     attn_part = jnp.einsum("tc,dc->td", context_low, out_low, preferred_element_type=jnp.float32)
-    attn_sum = lax.psum(attn_part, "tensor")
+    attn_sum = jnp.sum(lax.all_gather(attn_part, "tensor"), axis=0)
     residual_one = tokens_in.astype(jnp.float32) + attn_sum + biases[2]
     normed = layer_norm(residual_one, gains[0], biases[3])
     normed_low = normed.astype(jnp.bfloat16)

time: 903 us -> 950 us (1.052)
  other arithmetic: 56.1 us -> 81.4 us
  local copies, waits for them, and re-layouts: 48.5 us -> 70.9 us
    all_gather x0 -> x1, waiting for transfers between devices: none -> 120 us  [on_device(): attn_sum = jnp.sum(lax.all_gather(attn_part, 'tensor'), axis=0)]
    psum x1 -> x0, waiting for transfers between devices: 94.5 us -> none  [on_device(): attn_sum = lax.psum(attn_part, 'tensor')]
    reduce_scatter x4, waiting for transfers between devices: 195 us -> 170 us  [on_device(): lax.psum_scatter(part, 'dp', scatter_dimension=0, tiled=True)]
    reduce_sum x0 -> x1, other arithmetic: none -> 10.4 us  [on_device(): attn_sum = jnp.sum(lax.all_gather(attn_part, 'tensor'), axis=0)]
    unnamed x136 -> x116, local copies, waits for them, and re-layouts: 16.7 us -> 19.8 us
  transfers between devices with their start and end apart: 11 -> 11, of which waited for: 11 -> 10; matrix products, arithmetic and copies ran while one was open for 8% -> 11% of each run, Pallas kernels for 0% -> 0%
where the time goes in v1:
time: 950 us; the launch traced here: 941 us
  waiting for transfers between devices  607 us (64%)
  matrix products  90.2 us (9%)
  other arithmetic  81.4 us (9%)
  blocking collectives  73.2 us (8%)
  local copies, waits for them, and re-layouts  70.9 us (7%)
  between operations  16.8 us (2%)
    reduce_scatter x4, waiting for transfers between devices, on_device(): lax.psum_scatter(part, 'dp', scatter_dimension=0, tiled=True)  170 us
    all_gather x1, waiting for transfers between devices, on_device(): attn_sum = jnp.sum(lax.all_gather(attn_part, 'tensor'), axis=0)  120 us
    psum x1, waiting for transfers between devices, on_device(): down_sum = lax.psum(down_part, 'tensor')  78.4 us
    psum x1, waiting for transfers between devices, on_device(): input_grad = lax.psum(d_entry_part, 'tensor') + spread(d_res_one)  57.9 us
    all_gather x1, waiting for transfers between devices, on_device(): lax.all_gather(change_rows[3], 'dp', axis=0, tiled=True)  53.1 us
    all_gather x1, waiting for transfers between devices, on_device(): lax.all_gather(change_rows[2], 'dp', axis=0, tiled=True)  50 us
    all_gather x1, waiting for transfers between devices, on_device(): lax.all_gather(change_rows[0], 'dp', axis=0, tiled=True)  45.9 us
    psum x1, blocking collectives, on_device(): lax.psum((grad_gains, grad_biases, grad_bias_in), ('dp', 'tensor'))  41 us
  transfers between devices with their start and end apart: 11, of which 10 were waited for; matrix products, arithmetic and copies ran while one was open for 11% of the time, Pallas kernels for 0%

profile of v1, /device:TPU:0, one launch (start us, length us, event | category | flops | bytes accessed | tf_op | source)
XLA Modules:
  0.0 940.8 jit_solution(17461849073562420085)
XLA Ops:
  36.4 5.7 fusion.20
  49.1 119.9 %all-gather.12.cloned.1.call-done = f32[6144,768]{1,0:T(8,128)} async-done(((f32[1536,768]{1,0:T(8,128)}), f32[6144,768]{1,0:T(8,128)}) %all-gather.12.cloned.1.call-update) | async-done | bytes 18874384 | tf_op jit(solution)/shard_map/all_gather | solution.py:103
  169.0 10.4 %reduce_sum.224 = f32[1536,768]{1,0:T(8,128)} reduce(f32[4,1536,768]{2,1,0:T(8,128)} %bitcast.206, f32[]{:T(128)} %constant.60.clone.1), dimensions={0}, to_apply=%region_2.3 | reduce | flops 3538944 | bytes 23592964 | tf_op jit(solution)/shard_map/reduce_sum | solution.py:103
  187.5 17.8 %fusion.18 = f32[1536,768]{1,0:T(8,128)} fusion(bf16[1536,768]{1,0:T(8,128)(2,1)} %fusion.14, f32[768]{0:T(1024)} %dynamic_slice.23, f32[768,768]{1,0:T(8,128)} %param.31, f32[768,768]{1,0:T(8,128)} %param.30), kind=kOutput, calls=%fused_computation.39 | convolution fusion | flops 3702915072 | bytes 11799552 | tf_op jit(solution)/shard_map/tf,df->td/dot_general | solution.py:109
  213.4 4.6 fusion.173
  221.0 78.4 %all-reduce.5.cloned.1.call-done = f32[1536,768]{1,0:T(8,128)} async-done(((f32[1536,768]{1,0:T(8,128)}), f32[1536,768]{1,0:T(8,128)}) %all-reduce.5.cloned.1.call-update) | async-done | bytes 4718608 | tf_op jit(solution)/shard_map/psum | solution.py:110
  299.5 5.3 fusion.166
  314.5 4.8 fusion.180
  324.1 31.8 %all-reduce.7.cloned.1.call-done = f32[240,768]{1,0:T(8,128)} async-done(((f32[240,768]{1,0:T(8,128)}), f32[240,768]{1,0:T(8,128)}) %all-reduce.7.cloned.1.call-update) | async-done | bytes 737296 | tf_op jit(solution)/shard_map/psum | solution.py:154
  387.2 4.4 fusion.181
  397.7 4.7 fusion.62
  406.4 6.3 convolution_bitcast_fusion
  417.0 47.0 %reduce-scatter.5.cloned.1.call-done = f32[96,3,192]{2,0,1:T(8,128)} async-done(((f32[768,3,192]{2,0,1:T(8,128)}), f32[96,3,192]{2,0,1:T(8,128)}) %reduce-scatter.5.cloned.1.call-update) | async-done | bytes 221200 | tf_op jit(solution)/shard_map/reduce_scatter | solution.py:230
  466.3 69.6 %reduce-scatter.9.cloned.1.call-done = f32[96,768]{1,0:T(8,128)} async-done(((f32[768,768]{1,0:T(8,128)}), f32[96,768]{1,0:T(8,128)}) %reduce-scatter.9.cloned.1.call-update) | async-done | bytes 294928 | tf_op jit(solution)/shard_map/reduce_scatter | solution.py:230
  550.2 4.0 add_convert_fusion
  554.2 53.1 %reduce-scatter.11.cloned.1.call-done = f32[96,768]{1,0:T(8,128)} async-done(((f32[768,768]{1,0:T(8,128)}), f32[96,768]{1,0:T(8,128)}) %reduce-scatter.11.cloned.1.call-update) | async-done | bytes 294928 | tf_op jit(solution)/shard_map/reduce_scatter | solution.py:230
  622.3 41.0 %all-reduce = (f32[2,768]{1,0:T(2,128)}, f32[6,768]{1,0:T(8,128)}, f32[3072]{0:T(1024)}) all-reduce(f32[2,768]{1,0:T(2,128)} %maximum_multiply_fusion, f32[6,768]{1,0:T(8,128)S(1)} %stack.88, f32[3072]{0:T(1024)} %copy-done.42), channel_id=1, replica_groups=mesh['dp'=8,'tensor'=4] {'dp','tensor'}, use_global_device_ids=true, to_apply=%region_27.28 | all-reduce | flops 9216 | bytes 73728 | tf_op jit(solution)/shard_map/psum | solution.py:223
  669.3 4.3 fusion.47
  675.3 32.3 %all_gather.21 = f32[768,192]{1,0:T(8,128)S(1)} all-gather(f32[96,192]{1,0:T(8,128)S(1)} %get-tuple-element.107), channel_id=1, replica_groups=mesh['dp'=8,'tensor'=4] {'dp'}, dimensions={0}, use_global_device_ids=true | all-gather | bytes 663552 | tf_op jit(solution)/shard_map/all_gather | solution.py:253
  710.3 57.9 %all-reduce.9.cloned.1.call-done = f32[1536,768]{1,0:T(8,128)} async-done(((f32[1536,768]{1,0:T(8,128)}), f32[1536,768]{1,0:T(8,128)}) %all-reduce.9.cloned.1.call-update) | async-done | bytes 4718608 | tf_op jit(solution)/shard_map/psum | solution.py:202
  768.2 6.6 bitcast_add_fusion
  777.4 45.9 %all-gather.6.cloned.1.call-done = f32[768,3,192]{2,0,1:T(8,128)} async-done(((f32[96,3,192]{2,0,1:T(8,128)}), f32[768,3,192]{2,0,1:T(8,128)}) %all-gather.6.cloned.1.call-update) | async-done | bytes 1769488 | tf_op jit(solution)/shard_map/all_gather | solution.py:252
  826.3 50.0 %all-gather.8.cloned.1.call-done = f32[768,768]{1,0:T(8,128)} async-done(((f32[96,768]{1,0:T(8,128)}), f32[768,768]{1,0:T(8,128)}) %all-gather.8.cloned.1.call-update) | async-done | bytes 2359312 | tf_op jit(solution)/shard_map/all_gather | solution.py:254
  876.3 53.1 %all-gather.10.cloned.1.call-done = f32[768,768]{1,0:T(8,128)} async-done(((f32[96,768]{1,0:T(8,128)}), f32[768,768]{1,0:T(8,128)}) %all-gather.10.cloned.1.call-update) | async-done | bytes 2359312 | tf_op jit(solution)/shard_map/all_gather | solution.py:255
  (258 shorter events, 165.2 us)
Async XLA Ops:
  7.2 302.0 %copy-start = (bf16[1536,768]{1,0:T(8,128)(2,1)S(1)}, bf16[1536,768]{1,0:T(8,128)(2,1)}, u32[]{:S(2)}) copy-start(bf16[1536,768]{1,0:T(8,128)(2,1)} %param.22) | copy-start | bytes 7077892
  7.2 161.8 %all-gather.12.cloned.1.call-start = ((), (), s32[]{:S(2)}) async-start(), calls=%async_computation.14 | async-start | bytes 23592960 | tf_op jit(solution)/shard_map/all_gather | solution.py:103
  14.4 169.6 %copy-start.43 = (f32[768]{0:T(1024)}, f32[768]{0:T(1024)S(1)}, u32[]{:S(2)}) copy-start(f32[768]{0:T(1024)S(1)} %get-tuple-element.118) | copy-start | bytes 9220
  46.2 253.3 %all-reduce.5.cloned.1.call-start = ((), (), s32[]{:S(2)}) async-start(), calls=%async_computation.4 | async-start | bytes 9437184 | tf_op jit(solution)/shard_map/psum | solution.py:110
  49.1 134.9 %copy-start.30 = (f32[768]{0:T(1024)}, f32[768]{0:T(1024)S(1)}, u32[]{:S(2)}) copy-start(f32[768]{0:T(1024)S(1)} %get-tuple-element.78) | copy-start | bytes 9220
  205.3 150.6 %all-reduce.7.cloned.1.call-start = ((), (), s32[]{:S(2)}) async-start(), calls=%async_computation.5 | async-start | bytes 1474560 | tf_op jit(solution)/shard_map/psum | solution.py:154
  208.1 194.4 %copy-start.34 = (pred[3,512]{1,0:T(4,128)(4,1)}, pred[3,512]{1,0:T(4,128)(4,1)S(1)}, u32[]{:S(2)}) copy-start(pred[3,512]{1,0:T(4,128)(4,1)S(1)} %select_compare_fusion) | copy-start | bytes 4612
  218.0 81.5 %copy-start.31 = (f32[768]{0:T(1024)S(1)}, f32[768]{0:T(1024)}, u32[]{:S(2)}) copy-start(f32[768]{0:T(1024)} %copy-done.30) | copy-start | bytes 9220
  218.0 81.5 %copy-start.33 = (f32[1536]{0:T(1024)S(1)}, f32[1536]{0:T(1024)}, u32[]{:S(2)}) copy-start(f32[1536]{0:T(1024)} %copy-done.32) | copy-start | bytes 18436
  218.0 81.5 %copy-start.39 = (f32[1536]{0:T(1024)S(1)}, f32[1536]{0:T(1024)}, u32[]{:S(2)}) copy-start(f32[1536]{0:T(1024)} %copy-done.38) | copy-start | bytes 18436
  218.0 81.5 %copy-start.44 = (f32[768]{0:T(1024)S(1)}, f32[768]{0:T(1024)}, u32[]{:S(2)}) copy-start(f32[768]{0:T(1024)} %copy-done.43) | copy-start | bytes 9220
  218.0 81.5 %copy-start.51 = (f32[768]{0:T(1024)S(1)}, f32[768]{0:T(1024)}, u32[]{:S(2)}) copy-start(f32[768]{0:T(1024)} %get-tuple-element.119) | copy-start | bytes 9220
  321.4 142.6 %reduce-scatter.5.cloned.1.call-start = ((), (), s32[]{:S(2)}) async-start(), calls=%async_computation.7 | async-start | bytes 2654208 | tf_op jit(solution)/shard_map/reduce_scatter | solution.py:230
  394.6 141.3 %reduce-scatter.9.cloned.1.call-start = ((), (), s32[]{:S(2)}) async-start(), calls=%async_computation.10 | async-start | bytes 2654208 | tf_op jit(solution)/shard_map/reduce_scatter | solution.py:230
  397.6 209.7 %reduce-scatter.11.cloned.1.call-start = ((), (), s32[]{:S(2)}) async-start(), calls=%async_computation.12 | async-start | bytes 2654208 | tf_op jit(solution)/shard_map/reduce_scatter | solution.py:230
  402.4 271.2 %reduce-scatter.7.cloned.1.call-start = ((), (), s32[]{:S(2)}) async-start(), calls=%async_computation.9 | async-start | bytes 884736 | tf_op jit(solution)/shard_map/reduce_scatter | solution.py:230
  406.2 362.0 %all-reduce.9.cloned.1.call-start = ((), (), s32[]{:S(2)}) async-start(), calls=%async_computation.6 | async-start | bytes 9437184 | tf_op jit(solution)/shard_map/psum | solution.py:202
  412.7 131.1 %copy-start.41 = (f32[3,80]{1,0:T(4,128)S(1)}, f32[3,80]{1,0:T(4,128)}, u32[]{:S(2)}) copy-start(f32[3,80]{1,0:T(4,128)} %copy-done.40) | copy-start | bytes 2884
  412.7 410.6 %all-gather.6.cloned.1.call-start = ((), (), s32[]{:S(2)}) async-start(), calls=%async_computation.8 | async-start | bytes 2654208 | tf_op jit(solution)/shard_map/all_gather | solution.py:252
  466.2 410.0 %all-gather.8.cloned.1.call-start = ((), (), s32[]{:S(2)}) async-start(), calls=%async_computation.11 | async-start | bytes 2654208 | tf_op jit(solution)/shard_map/all_gather | solution.py:254
  538.2 391.2 %all-gather.10.cloned.1.call-start = ((), (), s32[]{:S(2)}) async-start(), calls=%async_computation.13 | async-start | bytes 2654208 | tf_op jit(solution)/shard_map/all_gather | solution.py:255
  550.2 113.1 %copy-start.37 = (f32[6,768]{1,0:T(8,128)S(1)}, f32[6,768]{1,0:T(8,128)}, u32[]{:S(2)}) copy-start(f32[6,768]{1,0:T(8,128)} %param.33) | copy-start | bytes 55300
  550.2 119.1 %copy-start.5 = (f32[240,768]{1,0:T(8,128)S(1)}, f32[240,768]{1,0:T(8,128)}, u32[]{:S(2)}) copy-start(f32[240,768]{1,0:T(8,128)} %copy-done.4) | copy-start | bytes 2211844
  550.2 119.1 %copy-start.35 = (pred[3,512]{1,0:T(4,128)(4,1)S(1)}, pred[3,512]{1,0:T(4,128)(4,1)}, u32[]{:S(2)}) copy-start(pred[3,512]{1,0:T(4,128)(4,1)} %copy-done.34) | copy-start | bytes 4612
  (41 other events, 417.9 us)
Sparse Core Ops, SparseCore 0:
  46.3 122.7 all-gather.11
  205.4 94.0 all-reduce.4
  321.5 34.3 all-reduce.6
  394.7 69.1 reduce-scatter.4
  467.9 67.9 reduce-scatter.8
  539.2 67.9 reduce-scatter.10
  611.2 61.4 reduce-scatter.6
  675.2 93.0 all-reduce.8
  771.2 52.0 all-gather.5
  825.6 50.5 all-gather.7
  878.7 50.5 all-gather.9
